TPU v7x, 32 devices: a whole 2x2x4 slice. The times are simulated.
32 devices in a mesh: groups: 2 (over y), ep: 16 (over z, x, core).
Axes of the slice: x: 2, y: 2, z: 4, core: 2. Of those that a mesh axis runs over, the one named last changes fastest.
Arguments:
- queries: bfloat16 [64, 128, 576], P(('groups', 'ep')), parts along dimension 0, may hold values from -120 to 120
- kv_cache: bfloat16 [64, 256, 576], P(('groups', 'ep')), parts along dimension 0, may hold values from -6 to 6
- kv_lengths: int32 [64], P(('groups', 'ep')), parts along dimension 0, may hold values from 32 to 256, as said below
- moe_input: bfloat16 [64, 7168], P(('groups', 'ep')), parts along dimension 0, may hold values from -6 to 6
- expert_ids: int32 [64, 8], P(('groups', 'ep')), parts along dimension 0, may hold values from 0 to 15, all different within a row; in each aligned block of 2 rows (0 to 1, 2 to 3, ...) at most 2 rows name the same one
- route_weights: float32 [64, 8], P(('groups', 'ep')), parts along dimension 0, may hold values from 0.1 to 1
- w_gate: bfloat16 [32768, 7168], P('ep'), may hold values from -0.0625 to 0.0625
- w_up: bfloat16 [32768, 7168], P('ep'), may hold values from -0.0625 to 0.0625
- w_down: bfloat16 [32768, 7168], P('ep'), may hold values from -0.125 to 0.125
Outputs:
- attended: bfloat16 [64, 128, 512], P(('groups', 'ep')), parts along dimension 0
- moe_output: bfloat16 [64, 7168], P(('groups', 'ep')), parts along dimension 0
There are 2 independent parts, one for each index of `groups`. A program takes and returns all parts, laid end to end along the dimension named above; an argument that names none is the same for every part. Nothing has to cross between parts.
Inputs may be any that keep to these rules, and one draw needn't show every extreme that they name: `expert_ids`: the 8 ids of a row differ. Among the 2 rows of one device no expert is named more than 2 times, and in every draw some expert is named exactly 2 times by the rows of some device. `kv_lengths`: some request in every draw uses all 256 slots.
All inputs are finite; a program needn't handle non-finite values.
Results may differ from a plain program's by a relative error of at most 0.0085.
Values may be sent and summed in bfloat16 or wider, within the bound.
A program may use at most 128 MiB of HBM per device.

v0:
```python
import jax
import jax.numpy as jnp
from jax import lax
from jax.sharding import PartitionSpec as P

LAT = 512
EXPERTS = 16
CAP = 2


score_scale = 192.0 ** (-0.5)


def attend_latent(queries, kv_cache, kv_lengths):
    scores = (
        jnp.einsum("rhk,rlk->rhl", queries, kv_cache, preferred_element_type=jnp.float32)
        * score_scale
    )
    slot_index = lax.broadcasted_iota(jnp.int32, scores.shape, 2)
    usable = slot_index < kv_lengths[:, None, None]
    scores = jnp.where(usable, scores, -1e30)
    row_max = jnp.max(scores, axis=2, keepdims=True)
    raw_weights = jnp.where(usable, jnp.exp(scores - row_max), 0.0)
    probs = (raw_weights / jnp.sum(raw_weights, axis=2, keepdims=True)).astype(jnp.bfloat16)
    values = kv_cache[:, :, :LAT]
    return jnp.einsum("rhl,rlk->rhk", probs, values, preferred_element_type=jnp.float32).astype(
        jnp.bfloat16
    )


def expert_rows(received, w_gate, w_up, w_down):
    flattened = received.reshape(-1, received.shape[-1])
    contract = (((1,), (1,)), ((), ()))
    gate_act = lax.dot_general(flattened, w_gate, contract, preferred_element_type=jnp.float32)
    up_act = lax.dot_general(flattened, w_up, contract, preferred_element_type=jnp.float32)
    hidden = (jax.nn.silu(gate_act) * up_act).astype(jnp.bfloat16)
    partial_out = jnp.dot(hidden, w_down, preferred_element_type=jnp.float32)
    return partial_out.reshape(received.shape[0], received.shape[1], partial_out.shape[-1])


def return_rows(partial_out):
    return lax.all_to_all(
        partial_out.astype(jnp.bfloat16), "ep", split_axis=0, concat_axis=0, tiled=True
    ).astype(partial_out.dtype)


def slot_map(member, capacity):
    position = jnp.cumsum(member, axis=-1) - member
    slot_ids = lax.broadcasted_iota(jnp.int32, (capacity, member.shape[-1]), 0)
    return member[..., None, :] * (position[..., None, :] == slot_ids).astype(jnp.int32)


def local(
    queries, kv_cache, kv_lengths, moe_input, expert_ids, route_weights, w_gate, w_up, w_down
):
    attended = attend_latent(queries, kv_cache, kv_lengths)
    devices = lax.axis_size("ep")
    slices = devices // EXPERTS
    requests = moe_input.shape[0]
    width = moe_input.shape[1]
    experts_iota = jnp.arange(EXPERTS, dtype=jnp.int32)
    matches = expert_ids[None, :, :] == experts_iota[:, None, None]
    member = jnp.sum(matches.astype(jnp.int32), axis=2)
    own_slots = slot_map(member, CAP)
    compact = jnp.einsum(
        "ecr,rd->ecd", own_slots.astype(jnp.bfloat16), moe_input, preferred_element_type=jnp.float32
    ).astype(jnp.bfloat16)
    outgoing = jnp.broadcast_to(compact[:, None], (EXPERTS, slices, CAP, width)).reshape(
        devices, CAP, width
    )
    returned = return_rows(
        expert_rows(
            lax.all_to_all(outgoing, "ep", split_axis=0, concat_axis=0, tiled=True),
            w_gate,
            w_up,
            w_down,
        )
    )
    summed = returned.reshape(EXPERTS, slices, CAP, width).sum(axis=1)
    weight_by_expert = jnp.sum(jnp.where(matches, route_weights[None, :, :], 0.0), axis=2)
    mixing = (own_slots.astype(jnp.float32) * weight_by_expert[:, None, :]).reshape(
        EXPERTS * CAP, requests
    )
    moe_output = lax.dot_general(
        mixing,
        summed.reshape(EXPERTS * CAP, width),
        (((0,), (0,)), ((), ())),
        precision=lax.Precision.HIGHEST,
        preferred_element_type=jnp.float32,
    )
    return (attended, moe_output.astype(jnp.bfloat16))


def solution(mesh):
    in_specs = (
        P(("groups", "ep"), None, None),
        P(("groups", "ep"), None, None),
        P(("groups", "ep")),
        P(("groups", "ep"), None),
        P(("groups", "ep"), None),
        P(("groups", "ep"), None),
        P("ep", None),
        P("ep", None),
        P("ep", None),
    )
    out_specs = (P(("groups", "ep"), None, None), P(("groups", "ep"), None))
    return jax.shard_map(local, mesh=mesh, in_specs=in_specs, out_specs=out_specs, check_vma=False)
```

profile of v0, /device:TPU:0, one launch (start us, length us, event | category | flops | bytes accessed | tf_op | source)
XLA Modules:
  0.0 79.0 jit_solution(7835878111630486628)
XLA Ops:
  0.6 0.0 copy-start
  0.6 0.8 %convert_reduce_fusion = s32[16,2]{0,1:T(2,128)S(1)} fusion(s32[2,8]{1,0:T(2,128)} %param.13), kind=kLoop, calls=%fused_computation.26 | loop fusion | flops 736 | bytes 192 | tf_op jit(solution)/shard_map/reduce_sum | solution.py:63
  1.5 1.1 %convolution_convert_fusion.1 = bf16[16,2,7168]{2,0,1:T(8,128)(2,1)S(1)} fusion(bf16[2,7168]{1,0:T(2,128)(2,1)} %param.12, s32[16,2]{0,1:T(2,128)S(1)} %convert_reduce_fusion, s32[16,2]{0,1:T(2,128)S(1)} %sub.17), kind=kOutput, calls=%fused_computation.2 | convolution fusion | flops 1147072 | bytes 487680 | tf_op jit(solution)/shard_map/ecr,rd->ecd/dot_general | solution.py:65
  2.6 0.5 copy.20
  3.1 20.4 %all_to_all.10 = bf16[16,2,7168]{2,1,0:T(2,128)(2,1)S(1)} all-to-all(bf16[16,2,7168]{2,1,0:T(2,128)(2,1)S(1)} %copy.20), channel_id=1, replica_groups=mesh['groups'=2,'ep'=16] {'ep'}, dimensions={0} | all-to-all | bytes 917504 | tf_op jit(solution)/shard_map/all_to_all | solution.py:73
  23.5 0.2 reshape.31
  23.6 14.0 %fusion.34 = f32[32,2048]{1,0:T(8,128)S(1)} fusion(bf16[32,7168]{1,0:T(8,128)(2,1)S(1)} %reshape.31, bf16[2048,7168]{1,0:T(8,128)(2,1)} %param.15), kind=kOutput, calls=%fused_computation.45 | convolution fusion | flops 939524096 | bytes 30081024 | tf_op jit(solution)/shard_map/dot_general | solution.py:34
  37.7 0.0 copy-start.2
  37.7 0.0 copy-start.3
  37.7 0.0 copy-start.1
  37.7 0.0 copy-start.4
  37.7 22.2 %convolution_convert_fusion = bf16[32,7168]{1,0:T(8,128)(2,1)S(1)} fusion(bf16[2048,7168]{1,0:T(8,128)(2,1)} %param.17, bf16[32,7168]{1,0:T(8,128)(2,1)S(1)} %reshape.31, bf16[2048,7168]{1,0:T(8,128)(2,1)} %param.16, f32[32,2048]{1,0:T(8,128)S(1)} %fusion.34), kind=kOutput, calls=%fused_computation.1 | convolution fusion | flops 1879670784 | bytes 59899904 | tf_op jit(solution)/shard_map/dot_general | solution.py:37
  59.9 0.9 %convert_element_type.40 = bf16[16,2,7168]{2,1,0:T(2,128)(2,1)} reshape(bf16[32,7168]{1,0:T(8,128)(2,1)S(1)} %convolution_convert_fusion) | data formatting | bytes 917504 | tf_op jit(solution)/shard_map/convert_element_type | solution.py:43
  60.9 3.9 %all-to-all-start.1 = ((bf16[16,2,7168]{2,1,0:T(2,128)(2,1)}), bf16[16,2,7168]{2,1,0:T(2,128)(2,1)S(1)}, u32[]{:S(2)}, u32[]{:S(2)}) async-start(bf16[16,2,7168]{2,1,0:T(2,128)(2,1)} %convert_element_type.40), calls=%async_computation.1 | async-start | bytes 917504 | tf_op jit(solution)/shard_map/all_to_all | solution.py:42
  64.8 0.0 copy-done.2
  64.8 0.0 copy-done.3
  64.8 0.1 select_reduce_fusion
  64.9 0.0 copy-done
  64.9 0.0 copy-done.1
  64.9 0.0 copy-done.4
  64.9 0.3 fusion.6
  65.2 0.2 fusion.33
  65.4 1.2 %convolution_convert_fusion.2 = bf16[2,128,512]{2,1,0:T(8,128)(2,1)} fusion(bf16[2,256,576]{1,2,0:T(8,128)(2,1)S(1)} %copy-done.1, f32[2,128]{1,0:T(2,128)S(1)} %fusion.33, f32[2,128,256]{2,1,0:T(8,128)S(1)} %fusion.6, s32[2]{0:T(128)S(1)} %copy-done.4), kind=kOutput, calls=%fused_computation.8 | convolution fusion | flops 67568128 | bytes 1312256 | tf_op jit(solution)/shard_map/rhl,rlk->rhk/dot_general | solution.py:26
  66.7 11.3 %all-to-all-done.1 = bf16[16,2,7168]{2,1,0:T(2,128)(2,1)S(1)} async-done(((bf16[16,2,7168]{2,1,0:T(2,128)(2,1)}), bf16[16,2,7168]{2,1,0:T(2,128)(2,1)S(1)}, u32[]{:S(2)}, u32[]{:S(2)}) %all-to-all-start.1) | async-done | bytes 458784 | tf_op jit(solution)/shard_map/all_to_all | solution.py:42
  78.0 1.0 %fusion.1 = bf16[2,7168]{1,0:T(2,128)(2,1)} fusion(bf16[16,2,7168]{2,1,0:T(2,128)(2,1)S(1)} %all-to-all-done.1, f32[16,2]{0,1:T(2,128)S(1)} %select_reduce_fusion, s32[16,2]{0,1:T(2,128)S(1)} %convert_reduce_fusion, s32[16,2]{0,1:T(2,128)S(1)} %sub.17), kind=kOutput, calls=%fused_computation.4 | convolution fusion | flops 5519616 | bytes 487808 | tf_op jit(solution)/shard_map/dot_general | solution.py:84
  (2 shorter events, 0.0 us)
Async XLA Ops:
  0.6 64.3 %copy-start = (bf16[2,128,576]{1,2,0:T(8,128)(2,1)S(1)}, bf16[2,128,576]{1,2,0:T(8,128)(2,1)}, u32[]{:S(2)}) copy-start(bf16[2,128,576]{1,2,0:T(8,128)(2,1)} %param.9) | copy-start | bytes 884740
  37.7 27.1 %copy-start.2 = (s32[2,8]{1,0:T(2,128)S(1)}, s32[2,8]{1,0:T(2,128)}, u32[]{:S(2)}) copy-start(s32[2,8]{1,0:T(2,128)} %param.13) | copy-start | bytes 196
  37.7 27.1 %copy-start.3 = (f32[2,8]{1,0:T(2,128)S(1)}, f32[2,8]{1,0:T(2,128)}, u32[]{:S(2)}) copy-start(f32[2,8]{1,0:T(2,128)} %param.14) | copy-start | bytes 196
  37.7 27.2 %copy-start.1 = (bf16[2,256,576]{1,2,0:T(8,128)(2,1)S(1)}, bf16[2,256,576]{1,2,0:T(8,128)(2,1)}, u32[]{:S(2)}) copy-start(bf16[2,256,576]{1,2,0:T(8,128)(2,1)} %param.10) | copy-start | bytes 1769476
  37.7 27.2 %copy-start.4 = (s32[2]{0:T(128)S(1)}, s32[2]{0:T(128)}, u32[]{:S(2)}) copy-start(s32[2]{0:T(128)} %param.11) | copy-start | bytes 28
  60.9 17.2 %all-to-all-start.1 = ((bf16[16,2,7168]{2,1,0:T(2,128)(2,1)}), bf16[16,2,7168]{2,1,0:T(2,128)(2,1)S(1)}, u32[]{:S(2)}, u32[]{:S(2)}) async-start(bf16[16,2,7168]{2,1,0:T(2,128)(2,1)} %convert_element_type.40), calls=%async_computation.1 | async-start | bytes 917504 | tf_op jit(solution)/shard_map/all_to_all | solution.py:42
where the time goes:
time: 79.3 us; the launch traced here: 79 us
  matrix products  39.8 us (50%)
  blocking collectives  20.4 us (26%)
  waiting for transfers between devices  11.3 us (14%)
  starting transfers between devices  3.89 us (5%)
  local copies, waits for them, and re-layouts  1.63 us (2%)
  other arithmetic  1.16 us (1%)
    dot_general x1, matrix products, expert_rows(): partial_out = jnp.dot(hidden, w_down, preferred_element_type=jnp.float32)  22.2 us
    all_to_all x1, blocking collectives, local(): lax.all_to_all(outgoing, 'ep', split_axis=0, concat_axis=0, tiled=True)  20.4 us
    dot_general x1, matrix products, expert_rows(): lax.dot_general(flattened, w_gate, contract, preferred_element_type=jnp.f...  14 us
    all_to_all x1, waiting for transfers between devices, return_rows(): lax.all_to_all(partial_out.astype(jnp.bfloat16), 'ep', split_axis=0, conc...  11.3 us
    all_to_all x1, starting transfers between devices, return_rows(): lax.all_to_all(partial_out.astype(jnp.bfloat16), 'ep', split_axis=0, conc...  3.89 us
  transfers between devices with their start and end apart: 1, of which 1 were waited for; matrix products, arithmetic and copies ran while one was open for 2% of the time, Pallas kernels for 0%

commit v1 on v0

v1 whole, which is shorter than its diff:
```python
import functools

import jax
import jax.numpy as jnp
from jax import lax
from jax.experimental import pallas as pl
from jax.experimental.pallas import tpu as pltpu
from jax.sharding import PartitionSpec as P

LAT = 512
EXPERTS = 16
LANES = 128
SCORE_SCALE = 192.0 ** (-0.5)
NT = (((1,), (1,)), ((), ()))
MAX_SLOTS = 14


def attend_one(query, cache, length):
    scores = lax.dot_general(query, cache, NT, preferred_element_type=jnp.float32) * SCORE_SCALE
    usable = lax.broadcasted_iota(jnp.int32, scores.shape, 1) < length
    scores = jnp.where(usable, scores, -1e30)
    row_max = jnp.max(scores, axis=1, keepdims=True)
    raw = jnp.where(usable, jnp.exp(scores - row_max), 0.0)
    probs = (raw / jnp.sum(raw, axis=1, keepdims=True)).astype(jnp.bfloat16)
    return jnp.dot(probs, cache[:, :LAT], preferred_element_type=jnp.float32)


def weight_lanes(ids, weights):
    lane = lax.broadcasted_iota(jnp.int32, (ids.shape[0], LANES), 1)
    expert, term = lane % EXPERTS, lane // EXPERTS
    dense = jnp.zeros(lane.shape, jnp.float32)
    for k in range(ids.shape[1]):
        dense += jnp.where(ids[:, k : k + 1] == expert, weights[:, k : k + 1], 0.0)
    high = dense.astype(jnp.bfloat16).astype(jnp.float32)
    rest = dense - high
    middle = rest.astype(jnp.bfloat16).astype(jnp.float32)
    low = rest - middle
    chosen = jnp.where(term == 0, high, jnp.where(term == 1, middle, low))
    return jnp.where(term < 3, chosen, 0.0).astype(jnp.bfloat16)


def kernel(
    n,
    slots,
    block,
    lengths,
    x_ref,
    ids_ref,
    route_ref,
    q_hbm,
    kv_hbm,
    wg_hbm,
    wu_hbm,
    wd_hbm,
    att_ref,
    out_ref,
    q_v,
    kv_v,
    ring,
    gathered,
    wide,
    xb,
    hid,
    mine,
    pair_out,
    pair_in,
    cross_out,
    cross_in,
    ring_sem,
    in_sem,
    x_send,
    x_recv,
    fwd_sem,
    pair_send,
    pair_recv,
    cross_send,
    cross_recv,
):
    me = lax.axis_index("ep")
    core = me % 2
    chip = me // 2
    chips = n // 2
    sibling = me + 1 - 2 * core
    req, width = x_ref.shape
    hidden = wg_hbm.shape[0]
    blocks = hidden // block
    cols = width // blocks
    half = chips * req
    expert = me // (n // EXPERTS)

    def peer(step):
        there = (chip + step) % chips
        return there, {"ep": there * 2 + core}

    def load_rows(source, row_block, slot):
        rows = pl.ds(pl.multiple_of(row_block * block, block), block)
        pltpu.make_async_copy(source.at[rows], ring.at[slot], ring_sem.at[slot]).start()

    def load_columns(part, slot):
        columns = pl.ds(pl.multiple_of(part * cols, LANES), cols)
        for b in range(blocks):
            pltpu.make_async_copy(
                wd_hbm.at[pl.ds(b * block, block), columns],
                ring.at[slot, :, pl.ds(b * cols, cols)],
                ring_sem.at[slot],
            ).start()

    def wait_slot(slot):
        pltpu.make_async_copy(wg_hbm.at[pl.ds(0, block)], ring.at[slot], ring_sem.at[slot]).wait()

    q_copy = pltpu.make_async_copy(q_hbm, q_v, in_sem.at[0])
    kv_copy = pltpu.make_async_copy(kv_hbm, kv_v, in_sem.at[1])
    q_copy.start()
    kv_copy.start()
    for i in range(slots):
        if i < 2 * blocks:
            load_rows(wg_hbm if i % 2 == 0 else wu_hbm, i // 2, i)
        else:
            load_columns(i - 2 * blocks, i)

    barrier = pltpu.get_barrier_semaphore()
    pl.semaphore_signal(
        barrier, inc=1, device_id={"ep": sibling}, device_id_type=pl.DeviceIdType.MESH
    )
    for step in range(1, chips):
        _, target = peer(step)
        pl.semaphore_signal(barrier, inc=1, device_id=target, device_id_type=pl.DeviceIdType.MESH)

    gathered[core, chip, :, pl.ds(0, width)] = x_ref[...]
    gathered[core, chip, :, pl.ds(width, LANES)] = weight_lanes(ids_ref[...], route_ref[...])
    pl.semaphore_wait(barrier, chips)

    def dispatch(step):
        _, target = peer(step)
        return pltpu.make_async_remote_copy(
            src_ref=gathered.at[core, chip],
            dst_ref=gathered.at[core, chip],
            send_sem=x_send,
            recv_sem=x_recv,
            device_id=target,
            device_id_type=pl.DeviceIdType.MESH,
        )

    for step in range(1, chips):
        dispatch(step).start()

    q_copy.wait()
    kv_copy.wait()
    for r in range(q_v.shape[0]):
        att_ref[r] = attend_one(q_v[r], kv_v[r], lengths[r]).astype(att_ref.dtype)

    others = gathered.at[core, pl.ds(0, chips - 1)]
    pltpu.make_async_copy(others, others, x_recv).wait()
    forward = pltpu.make_async_remote_copy(
        src_ref=gathered.at[core],
        dst_ref=gathered.at[core],
        send_sem=fwd_sem.at[0],
        recv_sem=fwd_sem.at[1],
        device_id={"ep": sibling},
        device_id_type=pl.DeviceIdType.MESH,
    )
    forward.start()
    for q in range(chips):
        wide[pl.ds(q * req, req), :] = gathered[core, q].astype(jnp.float32)
    forward.wait()
    for q in range(chips):
        wide[pl.ds(half + q * req, req), :] = gathered[1 - core, q].astype(jnp.float32)
    xb[...] = wide[:, :width].astype(jnp.bfloat16)
    lanes = wide[:, width:]
    lane = lax.broadcasted_iota(jnp.int32, lanes.shape, 1)
    share = jnp.sum(jnp.where(lane % EXPERTS == expert, lanes, 0.0), axis=1, keepdims=True)

    def gate_up(b, carry):
        first = (2 * b) % slots
        second = (2 * b + 1) % slots
        wait_slot(first)
        gate = lax.dot_general(xb[...], ring[first], NT, preferred_element_type=jnp.float32)
        wait_slot(second)
        up = lax.dot_general(xb[...], ring[second], NT, preferred_element_type=jnp.float32)
        hid[b] = (gate / (1.0 + jnp.exp(-gate)) * up).astype(jnp.bfloat16)
        ahead = 2 * b + slots

        @pl.when(ahead < 2 * blocks)
        def _():
            load_rows(wg_hbm, b + slots // 2, first)
            load_rows(wu_hbm, b + slots // 2, second)

        @pl.when(jnp.logical_and(ahead >= 2 * blocks, ahead < 3 * blocks))
        def _():
            load_columns(ahead - 2 * blocks, first)

        @pl.when(jnp.logical_and(ahead >= 2 * blocks, ahead + 1 < 3 * blocks))
        def _():
            load_columns(ahead + 1 - 2 * blocks, second)

        return carry

    lax.fori_loop(0, blocks, gate_up, 0)

    def pair_copy(c):
        return pltpu.make_async_remote_copy(
            src_ref=pair_out.at[c],
            dst_ref=pair_in.at[c],
            send_sem=pair_send.at[c],
            recv_sem=pair_recv.at[c],
            device_id={"ep": sibling},
            device_id_type=pl.DeviceIdType.MESH,
        )

    def send_on(c):
        pair_copy(c).wait_recv()
        total = (mine[c] + pair_in[c].astype(jnp.float32)).astype(jnp.bfloat16)
        total = total.astype(jnp.float32)
        for q in range(chips):
            cross_out[c, q] = total[q * req : (q + 1) * req].astype(jnp.bfloat16)
        for step in range(1, chips):
            there, target = peer(step)
            pltpu.make_async_remote_copy(
                src_ref=cross_out.at[c, there],
                dst_ref=cross_in.at[c, step - 1],
                send_sem=cross_send.at[c],
                recv_sem=cross_recv.at[c],
                device_id=target,
                device_id_type=pl.DeviceIdType.MESH,
            ).start()

    def down(c, carry):
        slot = (2 * blocks + c) % slots
        wait_slot(slot)
        product = jnp.zeros((2 * half, cols), jnp.float32)
        for b in range(blocks):
            product += jnp.dot(
                hid[b], ring[slot, :, b * cols : (b + 1) * cols], preferred_element_type=jnp.float32
            )
        product = product * share
        mine[c] = product[:half]
        pair_out[c] = product[half:].astype(jnp.bfloat16)
        pair_copy(c).start()

        @pl.when(c > 0)
        def _():
            send_on(c - 1)

        ahead = c + slots

        @pl.when(ahead < blocks)
        def _():
            load_columns(ahead, slot)

        return carry

    lax.fori_loop(0, blocks, down, 0)
    send_on(blocks - 1)

    for c in range(blocks):
        arrived = cross_in.at[c]
        pltpu.make_async_copy(arrived, arrived, cross_recv.at[c]).wait()
        total = cross_out[c, chip].astype(jnp.float32)
        for s in range(chips - 1):
            total += cross_in[c, s].astype(jnp.float32)
        out_ref[:, pl.ds(c * cols, cols)] = total.astype(out_ref.dtype)

    pltpu.make_async_copy(others, others, x_send).wait()
    for c in range(blocks):
        pair_copy(c).wait_send()
        sent = cross_out.at[c, pl.ds(0, chips - 1)]
        pltpu.make_async_copy(sent, sent, cross_send.at[c]).wait()


def local(n, queries, kv_cache, kv_lengths, moe_input, expert_ids, route_weights, wg, wu, wd):
    req, width = moe_input.shape
    hidden = wg.shape[0]
    block = min(256, hidden)
    blocks = hidden // block
    cols = width // blocks
    slots = min(MAX_SLOTS, 2 * ((3 * blocks) // 2))
    slots = max(slots, 2)
    chips = n // 2
    rows = n * req
    half = rows // 2
    bf16, f32 = jnp.bfloat16, jnp.float32
    vmem = pl.BlockSpec(memory_space=pltpu.VMEM)
    hbm = pl.BlockSpec(memory_space=pl.ANY)
    return pl.pallas_call(
        functools.partial(kernel, n, slots, block),
        out_shape=(
            jax.ShapeDtypeStruct(queries.shape[:2] + (LAT,), bf16),
            jax.ShapeDtypeStruct((req, width), bf16),
        ),
        in_specs=[pl.BlockSpec(memory_space=pltpu.SMEM)] + [vmem] * 3 + [hbm] * 5,
        out_specs=(vmem, vmem),
        scratch_shapes=[
            pltpu.VMEM(queries.shape, bf16),
            pltpu.VMEM(kv_cache.shape, bf16),
            pltpu.VMEM((slots, block, width), bf16),
            pltpu.VMEM((2, chips, req, width + LANES), bf16),
            pltpu.VMEM((rows, width + LANES), f32),
            pltpu.VMEM((rows, width), bf16),
            pltpu.VMEM((blocks, rows, block), bf16),
            pltpu.VMEM((blocks, half, cols), f32),
            pltpu.VMEM((blocks, half, cols), bf16),
            pltpu.VMEM((blocks, half, cols), bf16),
            pltpu.VMEM((blocks, chips, req, cols), bf16),
            pltpu.VMEM((blocks, chips - 1, req, cols), bf16),
            pltpu.SemaphoreType.DMA((slots,)),
            pltpu.SemaphoreType.DMA((2,)),
            pltpu.SemaphoreType.DMA,
            pltpu.SemaphoreType.DMA,
            pltpu.SemaphoreType.DMA((2,)),
            pltpu.SemaphoreType.DMA((blocks,)),
            pltpu.SemaphoreType.DMA((blocks,)),
            pltpu.SemaphoreType.DMA((blocks,)),
            pltpu.SemaphoreType.DMA((blocks,)),
        ],
        compiler_params=pltpu.CompilerParams(
            collective_id=0, has_side_effects=True, vmem_limit_bytes=58 * 2**20
        ),
    )(kv_lengths, moe_input, expert_ids, route_weights, queries, kv_cache, wg, wu, wd)


def solution(mesh):
    in_specs = (
        P(("groups", "ep"), None, None),
        P(("groups", "ep"), None, None),
        P(("groups", "ep")),
        P(("groups", "ep"), None),
        P(("groups", "ep"), None),
        P(("groups", "ep"), None),
        P("ep", None),
        P("ep", None),
        P("ep", None),
    )
    out_specs = (P(("groups", "ep"), None, None), P(("groups", "ep"), None))
    n = mesh.shape["ep"]
    return jax.shard_map(
        functools.partial(local, n), mesh=mesh, in_specs=in_specs, out_specs=out_specs, check_vma=False
    )
```

time: 79.3 us -> 74.5 us (0.939)
  Pallas kernels: 0 us -> 66.4 us
  matrix products: 39.8 us -> 0 us
  blocking collectives: 20.4 us -> 0 us
  waiting for transfers between devices: 11.3 us -> 0 us
  local copies, waits for them, and re-layouts: 1.63 us -> 7.06 us
  starting transfers between devices: 3.89 us -> 0 us
  other arithmetic: 1.16 us -> 0 us
    pallas_call x0 -> x1, Pallas kernels: none -> 66.4 us  [local(): pl.pallas_call(functools.partial(kernel, n, slots, block), out_shape=(jax...]
    dot_general x6 -> x0, matrix products: 39.8 us -> none  [the longest x1 22.2 us: expert_rows(): partial_out = jnp.dot(hidden, w_down, preferred_element_type=jnp.float32)]
    all_to_all x1 -> x0, blocking collectives: 20.4 us -> none  [local(): lax.all_to_all(outgoing, 'ep', split_axis=0, concat_axis=0, tiled=True)]
    all_to_all x1 -> x0, waiting for transfers between devices: 11.3 us -> none  [return_rows(): lax.all_to_all(partial_out.astype(jnp.bfloat16), 'ep', split_axis=0, conc...]
    unnamed x10 -> x4, local copies, waits for them, and re-layouts: 0.04 us -> 7.06 us
    all_to_all x1 -> x0, starting transfers between devices: 3.89 us -> none  [return_rows(): lax.all_to_all(partial_out.astype(jnp.bfloat16), 'ep', split_axis=0, conc...]
    convert_element_type x2 -> x0, local copies, waits for them, and re-layouts: 1.42 us -> none  [the longest x1 0.94 us: return_rows(): partial_out.astype(jnp.bfloat16)]
    reduce_sum x2 -> x0, other arithmetic: 0.9 us -> none  [the longest x1 0.81 us: local(): member = jnp.sum(matches.astype(jnp.int32), axis=2)]
  transfers between devices with their start and end apart: 1 -> 0, of which waited for: 1 -> 0; matrix products, arithmetic and copies ran while one was open for 2% -> 0% of each run, Pallas kernels for 0% -> 0%
where the time goes in v1:
time: 74.5 us; the launch traced here: 74.1 us
  Pallas kernels  66.4 us (89%)
  local copies, waits for them, and re-layouts  7.06 us (9%)
    pallas_call x1, Pallas kernels, local(): pl.pallas_call(functools.partial(kernel, n, slots, block), out_shape=(jax...  66.4 us
    unnamed x4, local copies, waits for them, and re-layouts  7.06 us

profile of v1, /device:TPU:0, one launch (start us, length us, event | category | flops | bytes accessed | tf_op | source)
XLA Modules:
  0.0 74.1 jit_solution(3107852610880070699)
XLA Ops:
  0.6 1.9 %copy.11.q_hbm = bf16[2,128,576]{2,1,0:T(8,128)(2,1)} copy(bf16[2,128,576]{1,2,0:T(8,128)(2,1)} %param.9) | data formatting | bytes 589824 | tf_op args[0]
  2.5 2.2 %copy.12.kv_hbm = bf16[2,256,576]{2,1,0:T(8,128)(2,1)} copy(bf16[2,256,576]{1,2,0:T(8,128)(2,1)} %param.10) | data formatting | bytes 1179648 | tf_op args[1]
  4.6 66.4 %shard_map.104 = (bf16[2,128,512]{2,1,0:T(8,128)(2,1)}, bf16[2,7168]{1,0:T(2,128)(2,1)}) custom-call(s32[2]{0:T(128)} %lengths.1, bf16[2,7168]{1,0:T(2,128)(2,1)} %x_ref.1, s32[2,8]{1,0:T(2,128)} %ids_ref.1, f32[2,8]{1,0:T(2,128)} %route_ref.1, bf16[2,128,576]{2,1,0:T(8,128)(2,1)} %copy.11.q_hbm, bf16[2,256,576]{2,1,0:T(8,128)(2,1)} %copy.12.kv_hbm, ...), custom_call_target="tpu_custom_call" | custom-call | tf_op jit(solution)/shard_map/pallas_call | solution.py:284
  71.1 1.7 %copy.15 = bf16[2,128,512]{2,1,0:T(8,128)(2,1)} copy(bf16[2,128,512]{2,1,0:T(8,128)(2,1)} %get-tuple-element.4) | data formatting | bytes 524288
  72.8 1.4 %copy.16 = bf16[2,7168]{1,0:T(2,128)(2,1)} copy(bf16[2,7168]{1,0:T(2,128)(2,1)} %get-tuple-element.5) | data formatting | bytes 57344

commit v2 on v1

--- a/solution.py
+++ b/solution.py
@@ -12,17 +12,18 @@
 LANES = 128
 SCORE_SCALE = 192.0 ** (-0.5)
 NT = (((1,), (1,)), ((), ()))
+TN = (((0,), (0,)), ((), ()))
 MAX_SLOTS = 14
 
 
 def attend_one(query, cache, length):
-    scores = lax.dot_general(query, cache, NT, preferred_element_type=jnp.float32) * SCORE_SCALE
+    scores = lax.dot_general(query, cache, TN, preferred_element_type=jnp.float32) * SCORE_SCALE
     usable = lax.broadcasted_iota(jnp.int32, scores.shape, 1) < length
     scores = jnp.where(usable, scores, -1e30)
     row_max = jnp.max(scores, axis=1, keepdims=True)
     raw = jnp.where(usable, jnp.exp(scores - row_max), 0.0)
     probs = (raw / jnp.sum(raw, axis=1, keepdims=True)).astype(jnp.bfloat16)
-    return jnp.dot(probs, cache[:, :LAT], preferred_element_type=jnp.float32)
+    return lax.dot_general(probs, cache[:LAT], NT, preferred_element_type=jnp.float32)
 
 
 def weight_lanes(ids, weights):
@@ -174,9 +175,10 @@
         first = (2 * b) % slots
         second = (2 * b + 1) % slots
         wait_slot(first)
-        gate = lax.dot_general(xb[...], ring[first], NT, preferred_element_type=jnp.float32)
         wait_slot(second)
-        up = lax.dot_general(xb[...], ring[second], NT, preferred_element_type=jnp.float32)
+        pair = ring[pl.ds(first, 2)].reshape(2 * block, width)
+        both = lax.dot_general(xb[...], pair, NT, preferred_element_type=jnp.float32)
+        gate, up = both[:, :block], both[:, block:]
         hid[b] = (gate / (1.0 + jnp.exp(-gate)) * up).astype(jnp.bfloat16)
         ahead = 2 * b + slots
 
@@ -268,6 +270,8 @@
 
 
 def local(n, queries, kv_cache, kv_lengths, moe_input, expert_ids, route_weights, wg, wu, wd):
+    heads = queries.shape[1]
+    queries, kv_cache = jnp.swapaxes(queries, 1, 2), jnp.swapaxes(kv_cache, 1, 2)
     req, width = moe_input.shape
     hidden = wg.shape[0]
     block = min(256, hidden)
@@ -284,7 +288,7 @@
     return pl.pallas_call(
         functools.partial(kernel, n, slots, block),
         out_shape=(
-            jax.ShapeDtypeStruct(queries.shape[:2] + (LAT,), bf16),
+            jax.ShapeDtypeStruct((queries.shape[0], heads, LAT), bf16),
             jax.ShapeDtypeStruct((req, width), bf16),
         ),
         in_specs=[pl.BlockSpec(memory_space=pltpu.SMEM)] + [vmem] * 3 + [hbm] * 5,

time: 74.5 us -> 56.2 us (0.75)
  Pallas kernels: 66.4 us -> 52.3 us
  local copies, waits for them, and re-layouts: 7.06 us -> 3.05 us
    pallas_call x1, Pallas kernels: 66.4 us -> 52.3 us  [local(): pl.pallas_call(functools.partial(kernel, n, slots, block), out_shape=(jax...]
    unnamed x4 -> x2, local copies, waits for them, and re-layouts: 7.06 us -> 3.05 us
where the time goes in v2:
time: 56.2 us; the launch traced here: 55.9 us
  Pallas kernels  52.3 us (93%)
  local copies, waits for them, and re-layouts  3.05 us (5%)
  between operations  0.64 us (1%)
    pallas_call x1, Pallas kernels, local(): pl.pallas_call(functools.partial(kernel, n, slots, block), out_shape=(jax...  52.3 us
    unnamed x2, local copies, waits for them, and re-layouts  3.05 us

profile of v2, /device:TPU:0, one launch (start us, length us, event | category | flops | bytes accessed | tf_op | source)
XLA Modules:
  0.0 55.9 jit_solution(9114604465153898205)
XLA Ops:
  0.6 52.3 %shard_map.104 = (bf16[2,128,512]{2,1,0:T(8,128)(2,1)}, bf16[2,7168]{1,0:T(2,128)(2,1)}) custom-call(s32[2]{0:T(128)} %lengths.1, bf16[2,7168]{1,0:T(2,128)(2,1)} %x_ref.1, s32[2,8]{1,0:T(2,128)} %ids_ref.1, f32[2,8]{1,0:T(2,128)} %route_ref.1, bf16[2,576,128]{2,1,0:T(8,128)(2,1)} %bitcast.3, bf16[2,576,256]{2,1,0:T(8,128)(2,1)} %bitcast.2, ...), custom_call_target="tpu_custom_call" | custom-call | tf_op jit(solution)/shard_map/pallas_call | solution.py:288
  52.9 1.7 %copy.13 = bf16[2,128,512]{2,1,0:T(8,128)(2,1)} copy(bf16[2,128,512]{2,1,0:T(8,128)(2,1)} %get-tuple-element.4) | data formatting | bytes 524288
  54.6 1.4 %copy.14 = bf16[2,7168]{1,0:T(2,128)(2,1)} copy(bf16[2,7168]{1,0:T(2,128)(2,1)} %get-tuple-element.5) | data formatting | bytes 57344

commit v3 on v2

--- a/solution.py
+++ b/solution.py
@@ -13,7 +13,8 @@
 SCORE_SCALE = 192.0 ** (-0.5)
 NT = (((1,), (1,)), ((), ()))
 TN = (((0,), (0,)), ((), ()))
-MAX_SLOTS = 14
+ROW_SLOTS = 8
+DOWN_SLOTS = 6
 
 
 def attend_one(query, cache, length):
@@ -42,7 +43,6 @@
 
 def kernel(
     n,
-    slots,
     block,
     lengths,
     x_ref,
@@ -58,6 +58,7 @@
     q_v,
     kv_v,
     ring,
+    down_ring,
     gathered,
     wide,
     xb,
@@ -68,6 +69,7 @@
     cross_out,
     cross_in,
     ring_sem,
+    down_sem,
     in_sem,
     x_send,
     x_recv,
@@ -86,6 +88,7 @@
     hidden = wg_hbm.shape[0]
     blocks = hidden // block
     cols = width // blocks
+    slots, down_slots = ring.shape[0], down_ring.shape[0]
     half = chips * req
     expert = me // (n // EXPERTS)
 
@@ -93,18 +96,23 @@
         there = (chip + step) % chips
         return there, {"ep": there * 2 + core}
 
+    barrier = pltpu.get_barrier_semaphore()
+    pl.semaphore_signal(
+        barrier, inc=1, device_id={"ep": sibling}, device_id_type=pl.DeviceIdType.MESH
+    )
+    for step in range(1, chips):
+        _, target = peer(step)
+        pl.semaphore_signal(barrier, inc=1, device_id=target, device_id_type=pl.DeviceIdType.MESH)
+
     def load_rows(source, row_block, slot):
         rows = pl.ds(pl.multiple_of(row_block * block, block), block)
         pltpu.make_async_copy(source.at[rows], ring.at[slot], ring_sem.at[slot]).start()
 
-    def load_columns(part, slot):
+    def column_copy(part, slot):
         columns = pl.ds(pl.multiple_of(part * cols, LANES), cols)
-        for b in range(blocks):
-            pltpu.make_async_copy(
-                wd_hbm.at[pl.ds(b * block, block), columns],
-                ring.at[slot, :, pl.ds(b * cols, cols)],
-                ring_sem.at[slot],
-            ).start()
+        return pltpu.make_async_copy(
+            wd_hbm.at[:, :, columns], down_ring.at[slot], down_sem.at[slot]
+        )
 
     def wait_slot(slot):
         pltpu.make_async_copy(wg_hbm.at[pl.ds(0, block)], ring.at[slot], ring_sem.at[slot]).wait()
@@ -114,18 +122,9 @@
     q_copy.start()
     kv_copy.start()
     for i in range(slots):
-        if i < 2 * blocks:
-            load_rows(wg_hbm if i % 2 == 0 else wu_hbm, i // 2, i)
-        else:
-            load_columns(i - 2 * blocks, i)
-
-    barrier = pltpu.get_barrier_semaphore()
-    pl.semaphore_signal(
-        barrier, inc=1, device_id={"ep": sibling}, device_id_type=pl.DeviceIdType.MESH
-    )
-    for step in range(1, chips):
-        _, target = peer(step)
-        pl.semaphore_signal(barrier, inc=1, device_id=target, device_id_type=pl.DeviceIdType.MESH)
+        load_rows(wg_hbm if i % 2 == 0 else wu_hbm, i // 2, i)
+    for c in range(down_slots):
+        column_copy(c, c).start()
 
     gathered[core, chip, :, pl.ds(0, width)] = x_ref[...]
     gathered[core, chip, :, pl.ds(width, LANES)] = weight_lanes(ids_ref[...], route_ref[...])
@@ -177,7 +176,7 @@
         wait_slot(first)
         wait_slot(second)
         pair = ring[pl.ds(first, 2)].reshape(2 * block, width)
-        both = lax.dot_general(xb[...], pair, NT, preferred_element_type=jnp.float32)
+        both = lax.dot_general(pair, xb[...], NT, preferred_element_type=jnp.float32).T
         gate, up = both[:, :block], both[:, block:]
         hid[b] = (gate / (1.0 + jnp.exp(-gate)) * up).astype(jnp.bfloat16)
         ahead = 2 * b + slots
@@ -186,14 +185,6 @@
         def _():
             load_rows(wg_hbm, b + slots // 2, first)
             load_rows(wu_hbm, b + slots // 2, second)
-
-        @pl.when(jnp.logical_and(ahead >= 2 * blocks, ahead < 3 * blocks))
-        def _():
-            load_columns(ahead - 2 * blocks, first)
-
-        @pl.when(jnp.logical_and(ahead >= 2 * blocks, ahead + 1 < 3 * blocks))
-        def _():
-            load_columns(ahead + 1 - 2 * blocks, second)
 
         return carry
 
@@ -211,8 +202,7 @@
 
     def send_on(c):
         pair_copy(c).wait_recv()
-        total = (mine[c] + pair_in[c].astype(jnp.float32)).astype(jnp.bfloat16)
-        total = total.astype(jnp.float32)
+        total = mine[c] + pair_in[c].astype(jnp.float32)
         for q in range(chips):
             cross_out[c, q] = total[q * req : (q + 1) * req].astype(jnp.bfloat16)
         for step in range(1, chips):
@@ -227,12 +217,12 @@
             ).start()
 
     def down(c, carry):
-        slot = (2 * blocks + c) % slots
-        wait_slot(slot)
+        slot = c % down_slots
+        column_copy(c, slot).wait()
         product = jnp.zeros((2 * half, cols), jnp.float32)
         for b in range(blocks):
             product += jnp.dot(
-                hid[b], ring[slot, :, b * cols : (b + 1) * cols], preferred_element_type=jnp.float32
+                hid[b], down_ring[slot, b], preferred_element_type=jnp.float32
             )
         product = product * share
         mine[c] = product[:half]
@@ -243,11 +233,11 @@
         def _():
             send_on(c - 1)
 
-        ahead = c + slots
+        ahead = c + down_slots
 
         @pl.when(ahead < blocks)
         def _():
-            load_columns(ahead, slot)
+            column_copy(ahead, slot).start()
 
         return carry
 
@@ -277,8 +267,7 @@
     block = min(256, hidden)
     blocks = hidden // block
     cols = width // blocks
-    slots = min(MAX_SLOTS, 2 * ((3 * blocks) // 2))
-    slots = max(slots, 2)
+    slots, down_slots = 2 * min(ROW_SLOTS // 2, blocks), min(DOWN_SLOTS, blocks)
     chips = n // 2
     rows = n * req
     half = rows // 2
@@ -286,7 +275,7 @@
     vmem = pl.BlockSpec(memory_space=pltpu.VMEM)
     hbm = pl.BlockSpec(memory_space=pl.ANY)
     return pl.pallas_call(
-        functools.partial(kernel, n, slots, block),
+        functools.partial(kernel, n, block),
         out_shape=(
             jax.ShapeDtypeStruct((queries.shape[0], heads, LAT), bf16),
             jax.ShapeDtypeStruct((req, width), bf16),
@@ -297,6 +286,7 @@
             pltpu.VMEM(queries.shape, bf16),
             pltpu.VMEM(kv_cache.shape, bf16),
             pltpu.VMEM((slots, block, width), bf16),
+            pltpu.VMEM((down_slots, blocks, block, cols), bf16),
             pltpu.VMEM((2, chips, req, width + LANES), bf16),
             pltpu.VMEM((rows, width + LANES), f32),
             pltpu.VMEM((rows, width), bf16),
@@ -307,6 +297,7 @@
             pltpu.VMEM((blocks, chips, req, cols), bf16),
             pltpu.VMEM((blocks, chips - 1, req, cols), bf16),
             pltpu.SemaphoreType.DMA((slots,)),
+            pltpu.SemaphoreType.DMA((down_slots,)),
             pltpu.SemaphoreType.DMA((2,)),
             pltpu.SemaphoreType.DMA,
             pltpu.SemaphoreType.DMA,
@@ -319,7 +310,10 @@
         compiler_params=pltpu.CompilerParams(
             collective_id=0, has_side_effects=True, vmem_limit_bytes=58 * 2**20
         ),
-    )(kv_lengths, moe_input, expert_ids, route_weights, queries, kv_cache, wg, wu, wd)
+    )(
+        kv_lengths, moe_input, expert_ids, route_weights, queries, kv_cache, wg, wu,
+        wd.reshape(blocks, block, width),
+    )
 
 
 def solution(mesh):

time: 56.2 us -> 53.5 us (0.952)
  Pallas kernels: 52.3 us -> 49.6 us
    pallas_call x1, Pallas kernels: 52.3 us -> 49.6 us  [local(): pl.pallas_call(functools.partial(kernel, n, block), out_shape=(jax.ShapeD...]
where the time goes in v3:
time: 53.5 us; the launch traced here: 53.2 us
  Pallas kernels  49.6 us (93%)
  local copies, waits for them, and re-layouts  3.05 us (6%)
  between operations  0.64 us (1%)
    pallas_call x1, Pallas kernels, local(): pl.pallas_call(functools.partial(kernel, n, block), out_shape=(jax.ShapeD...  49.6 us
    unnamed x2, local copies, waits for them, and re-layouts  3.05 us

profile of v3, /device:TPU:0, one launch (start us, length us, event | category | flops | bytes accessed | tf_op | source)
XLA Modules:
  0.0 53.2 jit_solution(4748196471792843384)
XLA Ops:
  0.6 49.6 %shard_map.104 = (bf16[2,128,512]{2,1,0:T(8,128)(2,1)}, bf16[2,7168]{1,0:T(2,128)(2,1)}) custom-call(s32[2]{0:T(128)} %lengths.1, bf16[2,7168]{1,0:T(2,128)(2,1)} %x_ref.1, s32[2,8]{1,0:T(2,128)} %ids_ref.1, f32[2,8]{1,0:T(2,128)} %route_ref.1, bf16[2,576,128]{2,1,0:T(8,128)(2,1)} %bitcast.5, bf16[2,576,256]{2,1,0:T(8,128)(2,1)} %bitcast.4, ...), custom_call_target="tpu_custom_call" | custom-call | tf_op jit(solution)/shard_map/pallas_call | solution.py:277
  50.2 1.7 %copy.13 = bf16[2,128,512]{2,1,0:T(8,128)(2,1)} copy(bf16[2,128,512]{2,1,0:T(8,128)(2,1)} %get-tuple-element.4) | data formatting | bytes 524288
  51.9 1.4 %copy.14 = bf16[2,7168]{1,0:T(2,128)(2,1)} copy(bf16[2,7168]{1,0:T(2,128)(2,1)} %get-tuple-element.5) | data formatting | bytes 57344
